TPU v7x, 256 devices: a whole 4x4x8 slice. The times are simulated.
256 devices in a mesh: tm: 32 (over y, x, core), panel: 8 (over z).
Axes of the slice: x: 4, y: 4, z: 8, core: 2. Of those that a mesh axis runs over, the one named last changes fastest.
Arguments:
- inv_diag: bfloat16 [32, 4096, 4096], P('tm', None, 'panel')
- couple: bfloat16 [32, 3, 4, 128, 128], P('tm'), may hold values from -0.25 to 0.25
- col_blocks: int32 [32, 3], replicated, may hold values from 0 to 31, as said below
- row_blocks: int32 [32, 4], P('tm'), may hold values from 0 to 31, as said below
Outputs:
- variances: float32 [32, 4096], P('tm', 'panel')
- schur: float32 [32, 384, 384], P('tm')
Inputs may be any that keep to these rules, and one draw needn't show every extreme that they name: Each row holds 4 different block numbers; row_blocks[0] holds 0 and 31. `col_blocks`: each row holds 3 different block numbers; for t >= 1 they are all among row_blocks[t - 1].
All inputs are finite; a program needn't handle non-finite values.
Results may differ from a plain program's by a relative error of at most 0.0003.
Values sent between devices are 32-bit elements; how exact they have to be, the bound alone decides.
A program may use at most 128 MiB of HBM per device.

v0:
```python
import jax
import jax.numpy as jnp
from jax import lax
from jax.sharding import PartitionSpec as P


def prefix(part, axis, combine, identity):
    count = lax.axis_size(axis)
    place = lax.axis_index(axis)
    ahead = count - 1 - place
    gathered = jax.tree.map(lambda a: lax.all_gather(a, axis), part)
    state = jax.tree.map(lambda a, e: jnp.zeros_like(a) + jnp.asarray(e, a.dtype), part, identity)

    def one(turn, state):
        source = count - 1 - turn
        return combine(
            state, jax.tree.map(lambda a: lax.dynamic_index_in_dim(a, source, 0, False), gathered)
        )

    return lax.fori_loop(0, ahead, one, state)


def matmul(left, right):
    return jnp.dot(left, right, precision=lax.Precision.HIGHEST, preferred_element_type=jnp.float32)


def compose(earlier, later):
    return (
        later[0] + matmul(later[1].T, matmul(earlier[0], later[1])),
        matmul(earlier[1], later[1]),
    )


def per_device(inv_diag, couple, col_blocks, row_blocks):
    steps = inv_diag.shape[0]
    nodes = inv_diag.shape[1]
    local = inv_diag.shape[2]
    coupled = couple.shape[1]
    block = couple.shape[3]
    width = coupled * block
    nblocks = nodes // block
    nlocal = local // block
    total_steps = col_blocks.shape[0]
    panel_first = lax.axis_index("panel") * nlocal
    step_first = lax.axis_index("tm") * steps
    local_ids = panel_first + jnp.arange(nlocal, dtype=jnp.int32)
    step = 0
    operand = inv_diag[step]
    hits = (row_blocks[step][:, None] == local_ids[None, :]).astype(jnp.bfloat16)
    spread = jnp.einsum("kb,ckij->bicj", hits, couple[step], preferred_element_type=jnp.float32)
    spread = spread.astype(jnp.bfloat16).reshape(local, width)
    later = jnp.minimum(step_first + step + 1, total_steps - 1)
    upcoming = lax.dynamic_index_in_dim(col_blocks, later, 0, keepdims=False)
    rows_here = lax.psum_scatter(
        jnp.dot(operand, spread, preferred_element_type=jnp.float32),
        "panel",
        scatter_dimension=0,
        tiled=True,
    )
    selector = (upcoming[:, None] == local_ids[None, :]).astype(jnp.float32)
    gram_part = matmul(rows_here.T, rows_here)
    link_part = jnp.einsum(
        "cb,biw->ciw",
        selector,
        rows_here.reshape(nlocal, block, width),
        precision=lax.Precision.HIGHEST,
    ).reshape(width, width)
    gram, link = lax.psum((gram_part, link_part), "panel")
    grams = [gram]
    links = [link]
    picks = [
        jnp.take(operand.reshape(nblocks, block, local), upcoming, axis=0)
        .reshape(width, local)
        .astype(jnp.float32)
    ]
    squares = [jnp.sum(jnp.square(operand.astype(jnp.float32)), axis=0)]
    combined = (grams[steps - 1], links[steps - 1])
    identity = (jnp.zeros((width, width), jnp.float32), jnp.eye(width, dtype=jnp.float32))
    incoming = prefix(combined, "tm", compose, identity)
    state = incoming[0]
    variances = [None] * steps
    handed = [None] * steps
    for step in reversed(range(steps)):
        variances[step] = squares[step] + jnp.sum(picks[step] * matmul(state, picks[step]), axis=0)
        state = grams[step] + matmul(links[step].T, matmul(state, links[step]))
        handed[step] = state
    return (jnp.stack(variances), jnp.stack(handed))


def solution(mesh):
    return jax.shard_map(
        per_device,
        mesh=mesh,
        in_specs=(P("tm", None, "panel"), P("tm", None, None, None, None), P(), P("tm", None)),
        out_specs=(P("tm", "panel"), P("tm", None, None)),
        check_vma=False,
    )
```

profile of v0, /device:TPU:32, one launch (start us, length us, event | category | flops | bytes accessed | tf_op | source)
XLA Modules:
  0.0 555.9 jit_solution(17525057297596688370)
XLA Ops:
  9.6 6.7 %convolution_bitcast_fusion = f32[4096,384]{0,1:T(8,128)} fusion(bf16[1,4096,512]{2,1,0:T(8,128)(2,1)} %param.6, bf16[48,8,4,128]{3,2,1,0:T(4,128)(2,1)S(1)} %bitcast.74), kind=kOutput, calls=%fused_computation.10 | convolution fusion | flops 1610612736 | bytes 10878976 | tf_op jit(solution)/shard_map/dot_general | solution.py:55
  16.5 75.9 %reduce-scatter.2.cloned.1.call-done = f32[512,384]{0,1:T(8,128)} async-done(((f32[4096,384]{0,1:T(8,128)}), f32[512,384]{0,1:T(8,128)}) %reduce-scatter.2.cloned.1.call-update) | async-done | bytes 786448 | tf_op jit(solution)/shard_map/reduce_scatter | solution.py:54
  95.8 3.6 fusion.24
  99.5 77.0 %all-reduce.3.cloned.1.call-done = (f32[384,384]{1,0:T(8,128)}, f32[384,384]{1,0:T(8,128)}) async-done(((f32[384,384]{1,0:T(8,128)}, f32[384,384]{1,0:T(8,128)}), (f32[384,384]{1,0:T(8,128)}, f32[384,384]{1,0:T(8,128)})) %all-reduce.3.cloned.1.call-update) | async-done | bytes 1179664 | tf_op jit(solution)/shard_map/psum | solution.py:68
  183.2 77.0 %all-gather.7.cloned.1.call-done = f32[12288,384]{1,0:T(8,128)} async-done(((f32[384,384]{1,0:T(8,128)}), f32[12288,384]{1,0:T(8,128)}) %all-gather.7.cloned.1.call-update) | async-done | bytes 18874384 | tf_op jit(solution)/shard_map/all_gather | solution.py:11
  260.3 84.5 %all-gather.5.cloned.1.call-done = f32[12288,384]{1,0:T(8,128)} async-done(((f32[384,384]{1,0:T(8,128)}), f32[12288,384]{1,0:T(8,128)}) %all-gather.5.cloned.1.call-update) | async-done | bytes 18874384 | tf_op jit(solution)/shard_map/all_gather | solution.py:11
  344.8 199.7 %while.14 = (s32[]{:T(128)}, f32[384,384]{1,0:T(8,128)S(1)}, s32[]{:T(128)}, f32[32,384,384]{2,1,0:T(8,128)}, f32[32,384,384]{2,1,0:T(8,128)}, /*index=5*/s32[]{:T(128)}, s32[]{:T(128)}, s32[]{:T(128)}, s32[]{:T(128)}) while((s32[]{:T(128)}, f32[384,384]{1,0:T(8,128)S(1)}, s32[]{:T(128)}, f32[32,384,384]{2,1,0:T(8,128)}, ...), condition=%wide.region_5.6_spmd, body=%wide.region_4.5_spmd.sunk | while | flops 1359101952 | bytes 4129935 | solution.py:20
  348.1 3.3 convolution_add_fusion.3
  354.5 3.3 convolution_add_fusion.3
  360.9 3.3 convolution_add_fusion.3
  367.4 3.3 convolution_add_fusion.3
  373.8 3.3 convolution_add_fusion.3
  380.2 3.3 convolution_add_fusion.3
  386.7 3.3 convolution_add_fusion.3
  399.5 3.3 convolution_add_fusion.3
  406.0 3.3 convolution_add_fusion.3
  425.3 3.3 convolution_add_fusion.3
  431.7 3.3 convolution_add_fusion.3
  457.4 3.3 convolution_add_fusion.3
  463.9 3.3 convolution_add_fusion.3
  489.6 3.3 convolution_add_fusion.3
  496.1 3.3 convolution_add_fusion.3
  521.8 3.3 convolution_add_fusion.3
  528.2 3.3 convolution_add_fusion.3
  (81 shorter events, 160.0 us)
Async XLA Ops:
  7.2 1.0 copy-start
  7.2 85.2 %reduce-scatter.2.cloned.1.call-start = ((), (), s32[]{:S(2)}) async-start(), calls=%async_computation.1 | async-start | bytes 7077888 | tf_op jit(solution)/shard_map/reduce_scatter | solution.py:54
  9.5 6.8 %copy-start.3 = (s32[32,3]{0,1:T(4,128)S(1)}, s32[32,3]{0,1:T(4,128)}, u32[]{:S(2)}) copy-start(s32[32,3]{0,1:T(4,128)} %param.8) | copy-start | bytes 1156
  16.3 160.2 %all-reduce.3.cloned.1.call-start = ((), (), s32[]{:S(2)}) async-start(), calls=%async_computation.4 | async-start | bytes 2359296 | tf_op jit(solution)/shard_map/psum | solution.py:68
  99.5 160.8 %all-gather.7.cloned.1.call-start = ((), (), s32[]{:S(2)}) async-start(), calls=%async_computation.3 | async-start | bytes 19464192 | tf_op jit(solution)/shard_map/all_gather | solution.py:11
  176.5 168.3 %all-gather.5.cloned.1.call-start = ((), (), s32[]{:S(2)}) async-start(), calls=%async_computation.2 | async-start | bytes 19464192 | tf_op jit(solution)/shard_map/all_gather | solution.py:11
  344.8 199.7 %copy-start.1 = (f32[384,384]{1,0:T(8,128)S(1)}, f32[384,384]{1,0:T(8,128)}, u32[]{:S(2)}) copy-start(f32[384,384]{1,0:T(8,128)} %get-tuple-element.98) | copy-start | bytes 1769476
  344.8 201.0 %copy-start.2 = (f32[384,384]{1,0:T(8,128)S(1)}, f32[384,384]{1,0:T(8,128)}, u32[]{:S(2)}) copy-start(f32[384,384]{1,0:T(8,128)} %get-tuple-element.97) | copy-start | bytes 1769476
Sparse Core Ops, SparseCore 0:
  16.4 75.9 reduce-scatter.1
  99.6 76.8 all-reduce.2
  179.0 81.1 all-gather.6
  262.7 82.0 all-gather.4
where the time goes:
time: 558 us; the launch traced here: 556 us
  waiting for transfers between devices  315 us (56%)
  matrix products  215 us (39%)
  between operations  13.9 us (2%)
  local copies, waits for them, and re-layouts  6.86 us (1%)
    dot_general x66, matrix products, matmul(): jnp.dot(left, right, precision=lax.Precision.HIGHEST, preferred_element_t...  206 us
    all_gather x2, waiting for transfers between devices, prefix(): gathered = jax.tree.map(lambda a: lax.all_gather(a, axis), part)  162 us
    psum x1, waiting for transfers between devices, per_device(): gram, link = lax.psum((gram_part, link_part), 'panel')  77 us
    reduce_scatter x1, waiting for transfers between devices, per_device(): lax.psum_scatter(jnp.dot(operand, spread, preferred_element_type=jnp.floa...  75.9 us
  transfers between devices with their start and end apart: 4, of which 4 were waited for; matrix products, arithmetic and copies ran while one was open for 1% of the time, Pallas kernels for 0%

commit v1 on v0

v1 whole, which is shorter than its diff:
```python
import functools

import jax
import jax.numpy as jnp
from jax import lax
from jax.experimental import pallas as pl
from jax.experimental.pallas import tpu as pltpu
from jax.sharding import PartitionSpec as P

MESH = pl.DeviceIdType.MESH
F32 = jnp.float32
BF16 = jnp.bfloat16

ROUTES = (
    (
        (15, 0, 0, -1, 3), (19, 0, 0, -1, 6), (26, 0, 0, 1, 20), (0, 0, 0, 0, 0), (4, 0, 0, 1, 8), (1, 0, 0, 0, 0),
        (2, 0, 0, 0, 0), (3, 0, 0, 0, 0), (22, 0, 0, -1, 9), (6, 0, 0, 1, 11), (30, 0, 0, -1, 11), (7, 0, 0, 1, 14),
        (23, 0, 0, -1, 14), (17, 0, 0, 1, 19), (5, 0, 1, 0, 0), (13, 0, 0, -1, 16), (18, 0, 0, 1, 22), (8, 0, 1, 0, 0),
        (29, 0, 0, -1, 20), (20, 0, 0, 1, 25), (9, 0, 1, 0, 0), (16, 0, 1, -1, 22), (25, 1, 0, 1, 24), (10, 0, 1, 0, 0),
        (12, 0, 0, -1, 27), (27, 0, 0, 1, 26), (11, 0, 1, 0, 0), (21, 0, 1, -1, 28), (28, 1, 0, 1, 29), (14, 1, 1, 0, 0),
        (24, 1, 1, 0, 0), (31, 1, 1, 0, 0),
    ),
    (
        (12, 0, 0, 1, 6), (13, 0, 0, 1, 10), (16, 0, 0, -1, 21), (21, 0, 0, -1, 27), (29, 0, 0, 1, 13), (5, 0, 0, -1, 14),
        (23, 0, 0, 1, 16), (8, 0, 1, -1, 17), (4, 1, 0, 0, 0), (22, 0, 0, 1, 18), (9, 0, 1, -1, 20), (6, 1, 0, 0, 0),
        (30, 0, 0, 1, 21), (10, 0, 1, -1, 23), (7, 1, 0, 0, 0), (15, 0, 0, 1, 23), (11, 0, 1, -1, 26), (19, 0, 0, 1, 26),
        (14, 0, 0, -1, 29), (17, 1, 1, 0, 0), (26, 1, 0, 1, 24), (24, 0, 1, -1, 30), (18, 1, 1, 0, 0), (31, 0, 0, -1, 31),
        (25, 1, 0, 1, 27), (20, 1, 1, 0, 0), (27, 1, 1, 0, 0), None, None, (28, 1, 1, 0, 0),
        None, None,
    ),
    (
        (14, 0, 0, 1, 3), (31, 0, 0, 1, 6), (8, 0, 0, -1, 7), (9, 0, 0, -1, 10), (21, 0, 0, 1, 9), (10, 0, 0, -1, 13),
        (12, 1, 0, 1, 11), (11, 0, 0, -1, 16), (16, 0, 0, 1, 14), (24, 0, 0, -1, 21), (13, 1, 0, 1, 16), (17, 0, 1, -1, 19),
        None, (29, 1, 0, 1, 19), (18, 0, 1, -1, 22), None, (23, 1, 0, 1, 22), (20, 0, 1, -1, 25),
        (22, 1, 0, 1, 25), (27, 0, 1, -1, 26), None, (30, 1, 0, 1, 27), (28, 0, 1, -1, 29), (15, 1, 1, 0, 0),
        (26, 1, 1, 0, 0), None, (19, 1, 1, 0, 0), (25, 1, 1, 0, 0), None, None,
        None, None,
    ),
    (
        (24, 0, 0, 1, 3), (25, 0, 0, -1, 27), None, (14, 1, 0, 1, 7), (17, 0, 1, -1, 11), None,
        (31, 1, 0, 1, 10), (18, 0, 1, -1, 14), None, (21, 1, 0, 1, 12), (20, 0, 1, -1, 17), (12, 1, 0, 1, 15),
        (28, 0, 1, -1, 22), None, (16, 1, 0, 1, 18), (27, 0, 1, -1, 19), (13, 1, 0, 1, 20), (26, 0, 1, -1, 24),
        None, (29, 1, 0, 1, 23), (15, 0, 1, -1, 23), None, (23, 1, 0, 1, 26), (19, 0, 1, -1, 26),
        None, (22, 1, 1, 0, 0), None, (30, 1, 1, 0, 0), None, None,
        None, None,
    ),
    (
        (25, 0, 0, 1, 3), (17, 0, 0, -1, 4), (18, 0, 0, -1, 7), (24, 1, 0, 1, 7), (20, 0, 1, -1, 10), None,
        (28, 0, 1, -1, 12), (14, 1, 0, 1, 11), None, (27, 0, 1, -1, 15), (31, 1, 0, 1, 15), (26, 0, 1, -1, 17),
        (21, 1, 0, 1, 16), None, None, (12, 1, 0, 1, 19), (15, 0, 1, -1, 20), None,
        (16, 1, 0, 1, 21), (19, 0, 1, -1, 23), (13, 1, 0, 1, 24), (22, 0, 1, -1, 25), None, (29, 1, 0, 1, 27),
        (30, 0, 1, -1, 27), None, (23, 1, 1, 0, 0), None, None, None,
        None, None,
    ),
    (
        (20, 0, 0, -1, 4), (28, 0, 0, -1, 6), None, (25, 1, 0, 1, 8), (27, 0, 1, -1, 9), None,
        (26, 0, 1, -1, 11), (24, 1, 0, 1, 11), None, None, None, (14, 1, 0, 1, 15),
        (15, 0, 1, -1, 16), None, (19, 0, 1, -1, 19), (31, 1, 0, 1, 19), (21, 1, 0, 1, 21), (22, 0, 1, -1, 21),
        None, (12, 1, 0, 1, 23), (30, 0, 1, -1, 24), (16, 1, 0, 1, 26), (23, 0, 1, -1, 26), None,
        (13, 1, 1, 0, 0), None, None, (29, 1, 1, 0, 0), None, None,
        None, None,
    ),
    (
        (27, 0, 0, -1, 4), (26, 0, 0, -1, 6), (28, 0, 0, 1, 4), None, None, None,
        None, (15, 0, 1, -1, 12), (25, 1, 0, 1, 12), None, (19, 0, 1, -1, 14), (24, 1, 0, 1, 15),
        (22, 0, 1, -1, 17), None, None, (14, 1, 0, 1, 19), (30, 0, 1, -1, 20), None,
        (23, 0, 1, -1, 22), (31, 1, 0, 1, 23), (13, 0, 1, -1, 24), (21, 1, 0, 1, 28), None, (12, 1, 0, 1, 27),
        (29, 0, 1, -1, 27), None, (16, 1, 1, 0, 0), None, None, None,
        None, None,
    ),
    (
        None, None, None, (15, 0, 1, -1, 7), (28, 1, 0, 1, 28), None,
        (19, 0, 1, -1, 10), None, None, (22, 0, 1, -1, 12), None, (30, 0, 1, -1, 16),
        (25, 1, 0, 1, 22), None, (23, 0, 1, -1, 18), (24, 1, 0, 1, 30), (13, 0, 1, -1, 20), None,
        None, (14, 1, 0, 1, 29), (29, 0, 1, -1, 24), None, (16, 0, 1, -1, 26), (31, 1, 0, 1, 31),
        None, None, None, (12, 1, 1, 0, 0), (21, 1, 1, 0, 0), None,
        None, None,
    ),
)
PAIRS = ((0, 0), (0, 1), (0, 2), (1, 1), (1, 2), (2, 2))


def pick(me, values):
    values = [int(v) for v in values]
    if len(set(values)) == 1:
        return values[0]
    out = jnp.int32(values[-1])
    for p in range(len(values) - 1):
        out = jnp.where(me == p, jnp.int32(values[p]), out)
    return out


def when(cond):
    if isinstance(cond, (bool, int)):
        return (lambda f: f()) if cond else (lambda f: None)
    return pl.when(cond)


def dot(a, b):
    return jnp.dot(a, b, preferred_element_type=F32)


def split(x):
    high = x.astype(BF16)
    return high, (x - high.astype(F32)).astype(BF16)


def kernel(ring, total_steps, inv, couple, cols, rows, var_out, schur_out, spread, picks, squares,
           out, got, link_part, link_full, link_put, link_got, keep_h, keep_l, keep_ht, keep_lt,
           b_put, b_got, a_now, a_put, a_got, mat_h, mat_l, tmp_h, tmp_l, last_put, last_got, last_full,
           state, state_full, send_sem, got_sem, lr_send, lr_recv, lg_send, lg_recv, fr_send, fr_recv,
           fg_send, fg_recv, st_send, st_recv, b_send, b_recv, br_send, a_send, a_recv, ar_send):
    me = lax.axis_index("panel")
    t = lax.axis_index("tm")
    m = t // 2
    core = lax.rem(t, 2)
    chips = total_steps // 2
    blk = couple.shape[2]
    local = inv.shape[2]
    width = 3 * blk
    nlocal = local // blk
    levels = len([d for d in (1, 2, 4, 8, 16) if d < chips])
    right = lax.rem(me + 1, ring)
    left = lax.rem(me + ring - 1, ring)
    mate = t + 1 - 2 * core

    def remote(src, dst, ssem, rsem, **where):
        return pltpu.make_async_remote_copy(src_ref=src, dst_ref=dst, send_sem=ssem, recv_sem=rsem,
                                            device_id=where, device_id_type=MESH)

    def arrived(dst, rsem):
        remote(dst, dst, rsem, rsem, tm=t, panel=me).wait_recv()

    def left_here(src, ssem):
        remote(src, src, ssem, ssem, tm=t, panel=me).wait_send()

    def mod(x):
        return lax.rem(x + 4 * ring, ring)

    barrier = pltpu.get_barrier_semaphore()
    greet = [(True, t, left), (True, t, right), (True, mate, me)]
    greet.append((jnp.logical_and(core == 1, t + 1 < total_steps), t + 1, me))
    greet.append((jnp.logical_and(core == 0, t > 0), t - 1, me))
    for k in range(levels):
        d = 2 ** k
        greet.append((jnp.logical_and(core == 0, m + d < chips), t + 2 * d, me))
        greet.append((jnp.logical_and(core == 0, m >= d), t - 2 * d, me))
    for cond, tt, pp in greet:
        @when(cond)
        def _(tt=tt, pp=pp):
            pl.semaphore_signal(barrier, inc=1, device_id=dict(tm=tt, panel=pp), device_id_type=MESH)

    for b in range(nlocal):
        for c in range(3):
            piece = jnp.zeros((blk, blk), F32)
            for k in range(4):
                off = rows[0, k] - (me * nlocal + b)
                piece = piece + couple[c, k].astype(F32) * (1 - jnp.minimum(off * off, 1)).astype(F32)
            spread[pl.ds(b * blk, blk), pl.ds(c * blk, blk)] = piece.astype(BF16)
    later = jnp.minimum(t + 1, total_steps - 1)
    for c in range(3):
        picks[pl.ds(c * blk, blk), :] = inv[cols[later, c]]
    for c in range(3):
        link_part[pl.ds(c * blk, blk), :] = dot(picks[pl.ds(c * blk, blk), :], spread[...])
    a_now[...] = jnp.zeros_like(a_now)

    peers = jnp.int32(0)
    for cond, tt, pp in greet:
        peers = peers + (1 if cond is True else cond.astype(jnp.int32))
    pl.semaphore_wait(barrier, peers)

    def reduce_step(s, part, size, put, recv, ssem, rsem):
        for way in range(2):
            if s >= 4 - way:
                continue
            nbr = right if way == 0 else left
            r = mod(me + 4 - s) if way == 0 else mod(me - 3 + s)
            src = part.at[pl.ds(pl.multiple_of(r * size, 8), size), :]
            j = 4 * way + s
            if s > 0:
                arrived(recv.at[j - 1], rsem.at[j - 1])
                put[j] = src[...] + recv[j - 1]
                src = put.at[j]
            remote(src, recv.at[j], ssem.at[j], rsem.at[j], panel=nbr).start()

    def reduce_end(part, size, recv, rsem, dest):
        arrived(recv.at[3], rsem.at[3])
        arrived(recv.at[6], rsem.at[6])
        at = pl.ds(pl.multiple_of(me * size, 8), size)
        dest[at, :] = part[at, :] + recv[3] + recv[6]

    def gather_step(s, dest, size, ssem, rsem, done):
        for way in range(2):
            if s >= 4 - way:
                continue
            nbr = right if way == 0 else left
            r = mod(me - s) if way == 0 else mod(me + s)
            at = pl.ds(pl.multiple_of(r * size, 8), size)
            j = 4 * way + s
            if s > 0:
                arrived(dest.at[at, :], rsem.at[j - 1])
            remote(dest.at[at, :], dest.at[at, :], ssem.at[j], rsem.at[j], panel=nbr).start()
            if done is not None and (s > 0 or way == 0):
                done(j, at)

    def gather_end(dest, size, rsem, done):
        for way in range(2):
            j = 3 + 3 * way
            r = mod(me - 4) if way == 0 else mod(me + 3)
            at = pl.ds(pl.multiple_of(r * size, 8), size)
            arrived(dest.at[at, :], rsem.at[j])
            if done is not None:
                done(4 + way * 3, at)

    def keep(v, x):
        h, l = split(x)
        keep_h[v] = h
        keep_l[v] = l
        xt = x.T
        h, l = split(xt)
        keep_ht[v] = h
        keep_lt[v] = l

    def times_kept(x, v):
        h, l = split(x)
        return dot(h, keep_h[v]) + dot(h, keep_l[v]) + dot(l, keep_h[v])

    def unpack(src, write):
        for n, (i, j) in enumerate(PAIRS):
            x = src[pl.ds(n * blk, blk), :]
            write(i, j, x)
            if i != j:
                write(j, i, x.T)

    def sandwich(src, v):
        def write(i, j, x):
            h, l = split(x)
            mat_h[pl.ds(i * blk, blk), pl.ds(j * blk, blk)] = h
            mat_l[pl.ds(i * blk, blk), pl.ds(j * blk, blk)] = l
        unpack(src, write)
        x = dot(mat_h[...], keep_h[v]) + dot(mat_h[...], keep_l[v]) + dot(mat_l[...], keep_h[v])
        h, l = split(x)
        tmp_h[...] = h
        tmp_l[...] = l
        n = 0
        for i in range(3):
            rows_i = pl.ds(i * blk, blk)
            cols_i = pl.ds(i * blk, width - i * blk)
            x = (dot(keep_ht[v, rows_i, :], tmp_h[:, cols_i]) + dot(keep_ht[v, rows_i, :], tmp_l[:, cols_i])
                 + dot(keep_lt[v, rows_i, :], tmp_h[:, cols_i]))
            for j in range(3 - i):
                at = pl.ds(n * blk, blk)
                a_now[at, :] = a_now[at, :] + x[:, j * blk:(j + 1) * blk]
                n += 1

    def add_squares(first, count):
        def one(n, total):
            x = inv[n].astype(F32)
            return total + jnp.sum((x * x).reshape(blk // 8, 8, local), axis=0)
        squares[...] = lax.fori_loop(first, first + count, one, squares[...])

    def basis_step(i):
        acts = [ROUTES[p][i] for p in range(ring)]
        active = pick(me, [a is not None for a in acts])
        acts = [a if a is not None else (0, 0, 0, 0, 0) for a in acts]
        steps = got.shape[0] // 2
        goes = pick(me, [a[3] != 0 for a in acts])
        is_root = pick(me, [a[3] == 0 for a in acts])

        @when(active == 1)
        def _():
            row = pick(me, [a[0] for a in acts])
            x = inv[row]
            out[i] = dot(x, spread[...])
            for side in range(2):
                @when(pick(me, [a[1 + side] for a in acts]) == 1)
                def _(side=side):
                    arrived(got.at[side * steps + i], got_sem.at[side * steps + i])
                    out[i] = out[i] + got[side * steps + i]

            @when(goes == 1)
            def _():
                slot = pick(me, [a[4] + (steps if a[3] < 0 else 0) for a in acts])
                to = pick(me, [(p + acts[p][3]) % ring for p in range(ring)])
                remote(out.at[i], got.at[slot], send_sem.at[i], got_sem.at[slot], panel=to).start()

            @when(is_root == 1)
            def _():
                x = out[i]
                h, l = split(x)
                th, tl = split(x.T)
                n = 0
                for b in range(3):
                    y = (dot(th[b * blk:(b + 1) * blk], h[:, b * blk:]) + dot(th[b * blk:(b + 1) * blk], l[:, b * blk:])
                         + dot(tl[b * blk:(b + 1) * blk], h[:, b * blk:]))
                    for j in range(3 - b):
                        at = pl.ds(n * blk, blk)
                        a_now[at, :] = a_now[at, :] + y[:, j * blk:(j + 1) * blk]
                        n += 1

    def b_first():
        @when(core == 1)
        def _():
            remote(link_full, b_got.at[0], b_send.at[0], b_recv.at[0], tm=mate).start()
        keep(0, link_full[...])

    def b_pair():
        @when(core == 0)
        def _():
            arrived(b_got.at[0], b_recv.at[0])
            x = times_kept(b_got[0], 0)
            keep(1, x)
            b_put[0] = x
        @when(core == 1)
        def _():
            keep_h[1] = keep_h[0]
            keep_l[1] = keep_l[0]
            keep_ht[1] = keep_ht[0]
            keep_lt[1] = keep_lt[0]

    def b_sends(k):
        d = 2 ** k
        return jnp.logical_and(core == 0, jnp.logical_and(m >= d, m + d < chips))

    def b_start(k):
        @when(b_sends(k))
        def _():
            remote(b_put.at[k], b_got.at[k + 1], b_send.at[k + 1], b_recv.at[k + 1], tm=t - 2 ** (k + 1)).start()

    def b_relays(k):
        return jnp.logical_and(core == 0, m + 2 ** (k + 1) < chips)

    def b_end(k):
        @when(m + 2 ** (k + 1) < chips)
        def _():
            arrived(b_got.at[k + 1], b_recv.at[k + 1])
            @when(core == 0)
            def _():
                remote(b_got.at[k + 1], b_got.at[k + 1], br_send.at[k], b_recv.at[k + 1], tm=mate).start()
            x = times_kept(b_got[k + 1], k + 1)
            keep(k + 2, x)
            if k + 2 < levels:
                b_put[k + 1] = x

    squares[...] = jnp.zeros_like(squares)
    nsteps = got.shape[0] // 2
    size = width // ring
    nblocks = inv.shape[0]
    extra = {}

    def add(i, f):
        extra.setdefault(i, []).append(f)

    for s in range(4):
        add(1 + s, functools.partial(reduce_step, s, link_part, size, link_put, link_got, lr_send, lr_recv))
    add(5, functools.partial(reduce_end, link_part, size, link_got, lr_recv, link_full))
    for s in range(4):
        add(5 + s, functools.partial(gather_step, s, link_full, size, lg_send, lg_recv, None))
    add(9, functools.partial(gather_end, link_full, size, lg_recv, None))
    add(9, b_first)
    add(10, b_pair)
    for k in range(levels - 1):
        add(10 + 4 * k, functools.partial(b_start, k))
        add(14 + 4 * k, functools.partial(b_end, k))
    for s in range(4):
        add(1 + s, functools.partial(add_squares, s * nblocks // 4, nblocks // 4))
    for i in range(max(nsteps, max(extra))+ 1):
        for f in extra.get(i, []):
            f()
        if i < nsteps:
            basis_step(i)

    @when(core == 1)
    def _():
        a_put[0] = a_now[...]
        remote(a_put.at[0], a_got.at[0], a_send.at[0], a_recv.at[0], tm=mate).start()

    @when(core == 0)
    def _():
        arrived(a_got.at[0], a_recv.at[0])
        sandwich(a_got.at[0], 0)

    for k in range(levels):
        d = 2 ** k
        @when(jnp.logical_and(core == 0, m >= d))
        def _(k=k, d=d):
            a_put[k + 1] = a_now[...]
            remote(a_put.at[k + 1], a_got.at[k + 1], a_send.at[k + 1], a_recv.at[k + 1], tm=t - 2 * d).start()

        @when(m + d < chips)
        def _(k=k):
            arrived(a_got.at[k + 1], a_recv.at[k + 1])
            @when(core == 0)
            def _():
                remote(a_got.at[k + 1], a_got.at[k + 1], ar_send.at[k], a_recv.at[k + 1], tm=mate).start()
            sandwich(a_got.at[k + 1], k + 1)

    size2 = 6 * blk // ring

    def forward(j, at):
        @when(t > 0)
        def _():
            remote(last_full.at[at, :], state.at[at, :], st_send.at[j], st_recv.at[j], tm=t - 1).start()

    for s in range(4):
        reduce_step(s, a_now, size2, last_put, last_got, fr_send, fr_recv)
    reduce_end(a_now, size2, last_got, fr_recv, last_full)
    for s in range(4):
        gather_step(s, last_full, size2, fg_send, fg_recv, forward)
    gather_end(last_full, size2, fg_recv, forward)

    def write_schur(i, j, x):
        schur_out[pl.ds(i * blk, blk), pl.ds(j * blk, blk)] = x
    unpack(last_full, write_schur)

    pieces = [mod(me - s) for s in range(4)] + [mod(me - 4)] + [mod(me + s) for s in range(1, 3)] + [mod(me + 3)]
    slots = [0, 1, 2, 3, 4, 5, 6, 7]

    @when(t + 1 < total_steps)
    def _():
        for j, r in zip(slots, pieces):
            at = pl.ds(pl.multiple_of(r * size2, 8), size2)
            arrived(state.at[at, :], st_recv.at[j])

    @when(t + 1 == total_steps)
    def _():
        state[...] = jnp.zeros_like(state)

    def write_state(i, j, x):
        h, l = split(x)
        mat_h[pl.ds(i * blk, blk), pl.ds(j * blk, blk)] = h
        mat_l[pl.ds(i * blk, blk), pl.ds(j * blk, blk)] = l
    unpack(state, write_state)
    total = jnp.sum(squares[...], axis=0, keepdims=True)
    y = dot(mat_h[...], picks[...]) + dot(mat_l[...], picks[...])
    var_out[...] = total + jnp.sum(picks[...].astype(F32) * y, axis=0, keepdims=True)

    for i in range(nsteps):
        acts = [ROUTES[p][i] or (0, 0, 0, 0, 0) for p in range(ring)]
        @when(pick(me, [a[3] != 0 for a in acts]) == 1)
        def _(i=i):
            left_here(out.at[i], send_sem.at[i])
    for j in range(7):
        left_here(link_got.at[j], lr_send.at[j])
        left_here(link_got.at[j], lg_send.at[j])
        left_here(last_got.at[j], fr_send.at[j])
        left_here(last_got.at[j], fg_send.at[j])

    @when(t > 0)
    def _():
        for j in range(8):
            left_here(last_got.at[0], st_send.at[j])

    @when(core == 1)
    def _():
        left_here(b_got.at[0], b_send.at[0])
        left_here(a_got.at[0], a_send.at[0])
    for k in range(levels):
        d = 2 ** k
        if k < levels - 1:
            @when(b_sends(k))
            def _(k=k):
                left_here(b_got.at[k + 1], b_send.at[k + 1])
            @when(b_relays(k))
            def _(k=k):
                left_here(b_got.at[k + 1], br_send.at[k])
        @when(jnp.logical_and(core == 0, m >= d))
        def _(k=k):
            left_here(a_got.at[k + 1], a_send.at[k + 1])
        @when(jnp.logical_and(core == 0, m + d < chips))
        def _(k=k):
            left_here(a_got.at[k + 1], ar_send.at[k])


def per_device(ring, inv_diag, couple, col_blocks, row_blocks):
    nodes, local = inv_diag.shape[1], inv_diag.shape[2]
    blk = couple.shape[3]
    width = couple.shape[1] * blk
    total_steps = col_blocks.shape[0]
    chips = total_steps // 2
    levels = len([d for d in (1, 2, 4, 8, 16) if d < chips])
    nsteps = max(len(r) for r in ROUTES)
    piece, piece2 = width // ring, 6 * blk // ring
    vm, dma = pltpu.VMEM, pltpu.SemaphoreType.DMA
    packed = (6 * blk, blk)
    scratch = [
        vm((local, width), BF16), vm((width, local), BF16), vm((8, local), F32),
        vm((nsteps, blk, width), F32), vm((2 * nsteps, blk, width), F32),
        vm((width, width), F32), vm((width, width), F32), vm((7, piece, width), F32), vm((7, piece, width), F32),
        vm((levels + 1, width, width), BF16), vm((levels + 1, width, width), BF16),
        vm((levels + 1, width, width), BF16), vm((levels + 1, width, width), BF16),
        vm((levels, width, width), F32), vm((levels, width, width), F32),
        vm(packed, F32), vm((levels + 1,) + packed, F32), vm((levels + 1,) + packed, F32),
        vm((width, width), BF16), vm((width, width), BF16), vm((width, width), BF16), vm((width, width), BF16),
        vm((7, piece2, blk), F32), vm((7, piece2, blk), F32), vm(packed, F32),
        vm(packed, F32), vm((8, 128), F32),
        dma((nsteps,)), dma((2 * nsteps,)),
        dma((7,)), dma((7,)), dma((7,)), dma((7,)), dma((7,)), dma((7,)), dma((7,)), dma((7,)),
        dma((8,)), dma((8,)),
        dma((levels,)), dma((levels,)), dma((levels,)),
        dma((levels + 1,)), dma((levels + 1,)), dma((levels,)),
    ]
    vmem = pl.BlockSpec(memory_space=pltpu.VMEM)
    smem = pl.BlockSpec(memory_space=pltpu.SMEM)
    variances, schur = pl.pallas_call(
        functools.partial(kernel, ring, total_steps),
        out_shape=(jax.ShapeDtypeStruct((1, local), F32), jax.ShapeDtypeStruct((width, width), F32)),
        in_specs=[vmem, vmem, smem, smem],
        out_specs=(vmem, vmem),
        scratch_shapes=scratch,
        compiler_params=pltpu.CompilerParams(
            collective_id=0, has_side_effects=True, vmem_limit_bytes=56 * 1024 * 1024
        ),
        name="sweep",
    )(inv_diag[0].reshape(nodes // blk, blk, local), couple[0], col_blocks, row_blocks)
    return variances, schur[None]


def solution(mesh):
    return jax.shard_map(
        functools.partial(per_device, mesh.shape["panel"]),
        mesh=mesh,
        in_specs=(P("tm", None, "panel"), P("tm", None, None, None, None), P(), P("tm", None)),
        out_specs=(P("tm", "panel"), P("tm", None, None)),
        check_vma=False,
    )
```

time: 558 us -> 160 us (0.29)
  the two profiles are of different devices: /device:TPU:32 before, /device:TPU:35 now
where the time goes in v1:
time: 160 us
  Pallas kernels  155 us (97%)
  local copies, waits for them, and re-layouts  4.54 us (3%)
    pallas_call x1, Pallas kernels, per_device(): pl.pallas_call(functools.partial(kernel, ring, total_steps), out_shape=(j...  155 us
    unnamed x3, local copies, waits for them, and re-layouts  4.54 us

profile of v1, /device:TPU:35, one launch (start us, length us, event | category | flops | bytes accessed | tf_op | source)
XLA Modules:
  0.0 159.9 jit_solution(2402238983726894194)
XLA Ops:
  0.6 1.4 copy.6.cols
  2.0 154.7 %sweep.1 = (f32[1,512]{1,0:T(1,128)}, f32[384,384]{1,0:T(8,128)}) custom-call(bf16[32,128,512]{2,1,0:T(8,128)(2,1)} %bitcast.3, bf16[3,4,128,128]{3,2,1,0:T(8,128)(2,1)} %bitcast.5, s32[32,3]{1,0:T(8,128)} %copy.6.cols, s32[1,4]{1,0:T(1,128)} %rows.1), custom_call_target="tpu_custom_call" | custom-call | tf_op jit(solution)/shard_map/sweep/pallas_call | solution.py:505
  156.7 1.3 copy.9
  158.0 1.9 %copy.10 = f32[1,384,384]{2,1,0:T(8,128)} copy(f32[1,384,384]{2,1,0:T(8,128)} %bitcast.4) | data formatting | bytes 1179648

commit v2 on v1

v2 whole, which is shorter than its diff:
```python
import functools

import jax
import jax.numpy as jnp
from jax import lax
from jax.experimental import pallas as pl
from jax.experimental.pallas import tpu as pltpu
from jax.sharding import PartitionSpec as P

MESH = pl.DeviceIdType.MESH
F32 = jnp.float32
BF16 = jnp.bfloat16

SPLIT = 1
ROUTES = (
    (
        (15, 0, 0, -1, 3, 0, 1), (26, 0, 0, 1, 23, 0, 1), (0, 0, 0, 0, 0, 0, 0), (1, 0, 0, 0, 1, 0, 0),
        (2, 0, 0, 0, 2, 0, 0), (3, 0, 0, 0, 3, 0, 0), (19, 0, 0, -1, 7, 0, 1), (4, 0, 0, 1, 8, 0, 1),
        (22, 0, 0, -1, 9, 0, 1), (6, 0, 0, 1, 11, 0, 1), (30, 0, 0, -1, 12, 0, 1), (7, 0, 0, 1, 14, 0, 1),
        (5, 0, 1, 0, 4, 0, 0), (23, 0, 0, -1, 14, 0, 1), (17, 0, 0, 1, 19, 0, 1), (8, 0, 1, 0, 5, 0, 0),
        (13, 0, 0, -1, 17, 0, 1), (18, 0, 0, 1, 22, 0, 1), (9, 0, 1, 0, 6, 0, 0), (29, 0, 0, -1, 20, 0, 1),
        (20, 0, 0, 1, 25, 0, 1), (10, 0, 1, 0, 7, 0, 0), (16, 0, 1, -1, 23, 0, 1), (25, 1, 0, 1, 26, 0, 1),
        (11, 0, 1, 0, 8, 0, 0), (12, 0, 0, -1, 26, 0, 1), (27, 0, 0, 1, 28, 0, 1), (21, 0, 1, -1, 28, 0, 1),
        (28, 1, 0, 1, 29, 0, 1), (14, 1, 1, 0, 9, 0, 0), (24, 1, 1, 0, 10, 0, 0), (31, 1, 1, 0, 11, 0, 0),
    ),
    (
        (12, 0, 0, 1, 4, 0, 1), (16, 0, 0, -1, 22, 0, 1), (13, 0, 0, 1, 12, 0, 1), (21, 0, 0, -1, 27, 0, 1),
        (29, 0, 0, 1, 14, 0, 1), (5, 0, 0, -1, 12, 0, 1), None, None,
        (4, 1, 0, 0, 0, 0, 0), (23, 0, 0, 1, 17, 0, 1), (8, 0, 1, -1, 15, 0, 1), (6, 1, 0, 0, 1, 0, 0),
        (22, 0, 0, 1, 19, 0, 1), (9, 0, 1, -1, 18, 0, 1), (7, 1, 0, 0, 2, 0, 0), (30, 0, 0, 1, 22, 0, 1),
        (10, 0, 1, -1, 21, 0, 1), (15, 0, 0, 1, 25, 0, 1), (11, 0, 1, -1, 24, 0, 1), (17, 1, 1, 0, 3, 0, 0),
        (19, 0, 0, 1, 26, 0, 1), (14, 0, 0, -1, 29, 0, 1), (18, 1, 1, 0, 4, 0, 0), (26, 1, 0, 1, 24, 0, 1),
        (24, 0, 1, -1, 30, 0, 1), (20, 1, 1, 0, 5, 0, 0), (25, 1, 0, 1, 27, 0, 1), (31, 0, 0, -1, 31, 0, 1),
        (27, 1, 1, 0, 6, 0, 0), (28, 1, 1, 0, 7, 0, 0), None, None,
    ),
    (
        (14, 0, 0, 1, 3, 0, 1), (8, 0, 0, -1, 10, 0, 1), (31, 0, 0, 1, 6, 0, 1), (9, 0, 0, -1, 13, 0, 1),
        (12, 1, 0, 1, 8, 0, 1), (10, 0, 0, -1, 16, 0, 1), None, (21, 0, 0, 1, 11, 0, 1),
        (11, 0, 0, -1, 18, 0, 1), (16, 0, 0, 1, 13, 0, 1), (24, 0, 0, -1, 24, 0, 1), None,
        (13, 1, 0, 1, 16, 0, 1), (17, 0, 1, -1, 19, 0, 1), (29, 1, 0, 1, 18, 0, 1), (18, 0, 1, -1, 22, 0, 1),
        None, (23, 1, 0, 1, 21, 0, 1), (20, 0, 1, -1, 25, 0, 1), (22, 1, 0, 1, 25, 0, 1),
        (27, 0, 1, -1, 28, 0, 1), None, (30, 1, 0, 1, 27, 0, 1), (28, 0, 1, -1, 29, 0, 1),
        (26, 1, 1, 0, 0, 0, 0), (15, 1, 1, 0, 1, 0, 0), (19, 1, 1, 0, 2, 0, 0), (25, 1, 1, 0, 3, 0, 0),
        None, None, None, None,
    ),
    (
        (24, 0, 0, 1, 3, 0, 1), (25, 0, 0, -1, 27, 0, 1), None, (14, 1, 0, 1, 8, 0, 1),
        (17, 0, 1, -1, 13, 0, 1), None, (31, 1, 0, 1, 10, 0, 1), (18, 0, 1, -1, 15, 0, 1),
        (12, 1, 0, 1, 13, 0, 1), (20, 0, 1, -1, 18, 0, 1), None, (21, 1, 0, 1, 16, 0, 1),
        (28, 0, 1, -1, 23, 0, 1), (16, 1, 0, 1, 17, 0, 1), (27, 0, 1, -1, 20, 0, 1), None,
        (13, 1, 0, 1, 21, 0, 1), (26, 0, 1, -1, 24, 0, 1), (29, 1, 0, 1, 22, 0, 1), (15, 0, 1, -1, 25, 0, 1),
        None, (23, 1, 0, 1, 25, 0, 1), (19, 0, 1, -1, 26, 0, 1), None,
        None, (22, 1, 1, 0, 0, 0, 0), None, (30, 1, 1, 0, 1, 0, 0),
        None, None, None, None,
    ),
    (
        (25, 0, 0, 1, 3, 0, 1), (17, 0, 0, -1, 4, 0, 1), (18, 0, 0, -1, 7, 0, 1), (24, 1, 0, 1, 8, 0, 1),
        (20, 0, 1, -1, 9, 0, 1), None, None, (28, 0, 1, -1, 12, 0, 1),
        (14, 1, 0, 1, 11, 0, 1), (27, 0, 1, -1, 14, 0, 1), (31, 1, 0, 1, 15, 0, 1), None,
        (26, 0, 1, -1, 17, 0, 1), (12, 1, 0, 1, 16, 0, 1), None, (15, 0, 1, -1, 19, 0, 1),
        (21, 1, 0, 1, 19, 0, 1), (16, 1, 0, 1, 21, 0, 1), (19, 0, 1, -1, 22, 0, 1), None,
        (22, 0, 1, -1, 25, 0, 1), (13, 1, 0, 1, 24, 0, 1), (29, 1, 0, 1, 26, 0, 1), (30, 0, 1, -1, 27, 0, 1),
        None, (23, 1, 1, 0, 0, 0, 0), None, None,
        None, None, None, None,
    ),
    (
        (20, 0, 0, -1, 4, 0, 1), None, (28, 0, 0, -1, 7, 0, 1), (25, 1, 0, 1, 8, 0, 1),
        (27, 0, 1, -1, 9, 0, 1), None, None, (26, 0, 1, -1, 12, 0, 1),
        (24, 1, 0, 1, 11, 0, 1), None, None, (14, 1, 0, 1, 15, 0, 1),
        (15, 0, 1, -1, 15, 0, 1), None, (19, 0, 1, -1, 18, 0, 1), (31, 1, 0, 1, 18, 0, 1),
        (12, 1, 0, 1, 20, 0, 1), (22, 0, 1, -1, 20, 0, 1), None, (21, 1, 0, 1, 23, 0, 1),
        (30, 0, 1, -1, 23, 0, 1), (16, 1, 0, 1, 25, 0, 1), (23, 0, 1, -1, 25, 0, 1), None,
        (13, 1, 1, 0, 0, 0, 0), None, (29, 1, 1, 0, 1, 0, 0), None,
        None, None, None, None,
    ),
    (
        (27, 0, 0, -1, 4, 0, 1), (28, 0, 0, 1, 4, 0, 1), (26, 0, 0, -1, 7, 0, 1), None,
        None, None, None, (15, 0, 1, -1, 12, 0, 1),
        (25, 1, 0, 1, 11, 0, 1), None, (19, 0, 1, -1, 14, 0, 1), (24, 1, 0, 1, 15, 0, 1),
        (22, 0, 1, -1, 17, 0, 1), None, None, (14, 1, 0, 1, 21, 0, 1),
        (30, 0, 1, -1, 20, 0, 1), (23, 0, 1, -1, 22, 0, 1), (31, 1, 0, 1, 24, 0, 1), None,
        (12, 1, 0, 1, 26, 0, 1), (13, 0, 1, -1, 24, 0, 1), (29, 0, 1, -1, 26, 0, 1), (21, 1, 0, 1, 28, 0, 1),
        None, (16, 1, 1, 0, 0, 0, 0), None, None,
        None, None, None, None,
    ),
    (
        None, None, None, (15, 0, 1, -1, 7, 0, 1),
        (28, 1, 0, 1, 28, 0, 1), None, None, (19, 0, 1, -1, 10, 0, 1),
        None, (22, 0, 1, -1, 12, 0, 1), None, (25, 1, 0, 1, 23, 0, 1),
        (30, 0, 1, -1, 16, 0, 1), None, (23, 0, 1, -1, 17, 0, 1), (24, 1, 0, 1, 30, 0, 1),
        None, (13, 0, 1, -1, 21, 0, 1), None, None,
        (29, 0, 1, -1, 22, 0, 1), (14, 1, 0, 1, 29, 0, 1), None, (16, 0, 1, -1, 25, 0, 1),
        (31, 1, 0, 1, 31, 0, 1), None, (12, 1, 1, 0, 0, 0, 0), None,
        (21, 1, 1, 0, 1, 0, 0), None, None, None,
    ),
)
LINK_AT = (0, 2, 4, 7, 10, 13, 15, 18, 20)
GRAM_AT = (
    (11, (0, 0, 0, 0, 0, 0, 0, 0), (2, 0, 0, 0, 0, 0, 0, 0)),
    (16, (2, 0, 0, 0, 0, 0, 0, 0), (3, 1, 0, 0, 0, 0, 0, 0)),
    (21, (3, 1, 0, 0, 0, 0, 0, 0), (3, 2, 0, 0, 0, 0, 0, 0)),
    (26, (3, 2, 0, 0, 0, 0, 0, 0), (4, 3, 1, 0, 0, 0, 0, 0)),
    (29, (4, 3, 1, 0, 0, 0, 0, 0), (4, 3, 2, 1, 0, 1, 0, 1)),
    (32, (4, 3, 2, 1, 0, 1, 0, 1), (6, 4, 2, 1, 1, 1, 1, 1)),
)
IDLE = (0, 0, 0, 0, 0, 0, 0)
PAIRS = ((0, 0), (0, 1), (0, 2), (1, 1), (1, 2), (2, 2))


def pick(me, values):
    values = [int(v) for v in values]
    if len(set(values)) == 1:
        return values[0]
    out = jnp.int32(values[-1])
    for p in range(len(values) - 1):
        out = jnp.where(me == p, jnp.int32(values[p]), out)
    return out


def when(cond):
    if isinstance(cond, (bool, int)):
        return (lambda f: f()) if cond else (lambda f: None)
    return pl.when(cond)


def dot(a, b):
    return jnp.dot(a, b, preferred_element_type=F32)


def split(x):
    high = x.astype(BF16)
    return high, (x - high.astype(F32)).astype(BF16)


def kernel(ring, total_steps, inv, couple, cols, rows, var_out, schur_out, spread, picks, squares,
           part, roots, got, link_part, link_full, link_put, link_got, keep_h, keep_l, keep_ht, keep_lt,
           b_put, b_got, a_now, a_put, a_got, mat_h, mat_l, tmp_h, tmp_l, last_got, last_full,
           state, state_full, send_sem, got_sem, lr_send, lr_recv, lg_send, lg_recv, fr_send, fr_recv,
           fg_send, fg_recv, st_send, st_recv, b_send, b_recv, br_send, a_send, a_recv, ar_send):
    me = lax.axis_index("panel")
    t = lax.axis_index("tm")
    m = t // 2
    core = lax.rem(t, 2)
    chips = total_steps // 2
    blk = couple.shape[2]
    local = inv.shape[2]
    width = 3 * blk
    half = blk // SPLIT
    nlocal = local // blk
    levels = len([d for d in (1, 2, 4, 8, 16) if d < chips])
    right = lax.rem(me + 1, ring)
    left = lax.rem(me + ring - 1, ring)
    mate = t + 1 - 2 * core

    def remote(src, dst, ssem, rsem, **where):
        return pltpu.make_async_remote_copy(src_ref=src, dst_ref=dst, send_sem=ssem, recv_sem=rsem,
                                            device_id=where, device_id_type=MESH)

    def arrived(dst, rsem):
        remote(dst, dst, rsem, rsem, tm=t, panel=me).wait_recv()

    def left_here(src, ssem):
        remote(src, src, ssem, ssem, tm=t, panel=me).wait_send()

    def mod(x):
        return lax.rem(x + 4 * ring, ring)

    barrier = pltpu.get_barrier_semaphore()
    greet = [(True, t, lax.rem(me + d, ring)) for d in range(1, ring)] + [(True, mate, me)]
    greet.append((jnp.logical_and(core == 1, t + 1 < total_steps), t + 1, me))
    greet.append((jnp.logical_and(core == 0, t > 0), t - 1, me))
    for k in range(levels):
        d = 2 ** k
        greet.append((jnp.logical_and(core == 0, m + d < chips), t + 2 * d, me))
        greet.append((jnp.logical_and(core == 0, m >= d), t - 2 * d, me))
    for cond, tt, pp in greet:
        @when(cond)
        def _(tt=tt, pp=pp):
            pl.semaphore_signal(barrier, inc=1, device_id=dict(tm=tt, panel=pp), device_id_type=MESH)

    for b in range(nlocal):
        for c in range(3):
            piece = jnp.zeros((blk, blk), F32)
            for k in range(4):
                off = rows[0, k] - (me * nlocal + b)
                piece = piece + couple[c, k].astype(F32) * (1 - jnp.minimum(off * off, 1)).astype(F32)
            spread[pl.ds(b * blk, blk), pl.ds(c * blk, blk)] = piece.astype(BF16)
    later = jnp.minimum(t + 1, total_steps - 1)
    for c in range(3):
        for n in range(SPLIT):
            picks[pl.ds(c * blk + n * half, half), :] = inv[SPLIT * cols[later, c] + n]
    for c in range(3):
        link_part[pl.ds(c * blk, blk), :] = dot(picks[pl.ds(c * blk, blk), :], spread[...])
    peers = jnp.int32(0)
    for cond, tt, pp in greet:
        peers = peers + (1 if cond is True else cond.astype(jnp.int32))
    pl.semaphore_wait(barrier, peers)

    def reduce_step(s, source, size, put, recv, ssem, rsem):
        for way in range(2):
            if s >= 4 - way:
                continue
            nbr = right if way == 0 else left
            r = mod(me + 4 - s) if way == 0 else mod(me - 3 + s)
            src = source.at[pl.ds(pl.multiple_of(r * size, 8), size), :]
            j = 4 * way + s
            if s > 0:
                arrived(recv.at[j - 1], rsem.at[j - 1])
                put[j] = src[...] + recv[j - 1]
                src = put.at[j]
            remote(src, recv.at[j], ssem.at[j], rsem.at[j], panel=nbr).start()

    def reduce_end(source, size, recv, rsem, dest):
        arrived(recv.at[3], rsem.at[3])
        arrived(recv.at[6], rsem.at[6])
        at = pl.ds(pl.multiple_of(me * size, 8), size)
        dest[at, :] = source[at, :] + recv[3] + recv[6]

    def gather_step(s, dest, size, ssem, rsem):
        for way in range(2):
            if s >= 4 - way:
                continue
            nbr = right if way == 0 else left
            r = mod(me - s) if way == 0 else mod(me + s)
            at = pl.ds(pl.multiple_of(r * size, 8), size)
            j = 4 * way + s
            if s > 0:
                arrived(dest.at[at, :], rsem.at[j - 1])
            remote(dest.at[at, :], dest.at[at, :], ssem.at[j], rsem.at[j], panel=nbr).start()

    def gather_end(dest, size, rsem):
        for way in range(2):
            r = mod(me - 4) if way == 0 else mod(me + 3)
            at = pl.ds(pl.multiple_of(r * size, 8), size)
            arrived(dest.at[at, :], rsem.at[3 + 3 * way])

    def spread_start(source, size, recv, ssem, rsem):
        for d in range(1, ring):
            r = lax.rem(me + d, ring)
            src = source.at[pl.ds(pl.multiple_of(r * size, 8), size), :]
            remote(src, recv.at[d - 1], ssem.at[d - 1], rsem.at[d - 1], panel=r).start()

    def spread_end(source, size, recv, rsem, dest):
        at = pl.ds(pl.multiple_of(me * size, 8), size)
        x = source[at, :]
        for d in range(1, ring):
            arrived(recv.at[d - 1], rsem.at[d - 1])
            x = x + recv[d - 1]
        dest[at, :] = x

    def share_start(dest, size, ssem, rsem):
        at = pl.ds(pl.multiple_of(me * size, 8), size)
        for d in range(1, ring):
            remote(dest.at[at, :], dest.at[at, :], ssem.at[d - 1], rsem.at[d - 1], panel=lax.rem(me + d, ring)).start()

    def share_end(dest, size, rsem, done):
        for d in (1, 7, 2, 6, 3, 5, 4):
            r = lax.rem(me + ring - d, ring)
            at = pl.ds(pl.multiple_of(r * size, 8), size)
            arrived(dest.at[at, :], rsem.at[d - 1])
            if done is not None:
                done(d, at)

    def halves(n):
        return [pl.ds(0, n // 2), pl.ds(n // 2, n // 2)]

    def ship(src, dst, ssem, rsem, n, h, **where):
        at = halves(src.shape[1])[h]
        remote(src.at[n, at, :], dst.at[n, at, :], ssem.at[n, h], rsem.at[n, h], **where).start()

    def landed(dst, rsem, n, h):
        arrived(dst.at[n, halves(dst.shape[1])[h], :], rsem.at[n, h])

    def shipped(src, ssem, n):
        for h in range(2):
            left_here(src.at[n, halves(src.shape[1])[h], :], ssem.at[n, h])

    def relay(buf, ssem, rsem, n):
        for h in range(2):
            landed(buf, rsem, n, h)
            @when(core == 0)
            def _(h=h):
                ship(buf, buf, ssem, rsem, n, h, tm=mate)

    def keep(v, x):
        h, l = split(x)
        keep_h[v] = h
        keep_l[v] = l
        xt = x.T
        h, l = split(xt)
        keep_ht[v] = h
        keep_lt[v] = l

    def times_kept(x, v):
        h, l = split(x)
        return dot(h, keep_h[v]) + dot(h, keep_l[v]) + dot(l, keep_h[v])

    def unpack(src, write):
        for n, (i, j) in enumerate(PAIRS):
            x = src[pl.ds(n * blk, blk), :]
            write(i, j, x)
            if i != j:
                write(j, i, x.T)

    def sandwich(src, v):
        def write(i, j, x):
            h, l = split(x)
            mat_h[pl.ds(i * blk, blk), pl.ds(j * blk, blk)] = h
            mat_l[pl.ds(i * blk, blk), pl.ds(j * blk, blk)] = l
        unpack(src, write)
        x = dot(mat_h[...], keep_h[v]) + dot(mat_h[...], keep_l[v]) + dot(mat_l[...], keep_h[v])
        h, l = split(x)
        tmp_h[...] = h
        tmp_l[...] = l
        n = 0
        for i in range(3):
            rows_i = pl.ds(i * blk, blk)
            cols_i = pl.ds(i * blk, width - i * blk)
            x = (dot(keep_ht[v, rows_i, :], tmp_h[:, cols_i]) + dot(keep_ht[v, rows_i, :], tmp_l[:, cols_i])
                 + dot(keep_lt[v, rows_i, :], tmp_h[:, cols_i]))
            for j in range(3 - i):
                at = pl.ds(n * blk, blk)
                a_now[at, :] = a_now[at, :] + x[:, j * blk:(j + 1) * blk]
                n += 1

    def add_squares(first, count):
        def one(n, total):
            x = inv[n].astype(F32)
            return total + jnp.sum((x * x).reshape(half // 8, 8, local), axis=0)
        squares[...] = lax.fori_loop(first, first + count, one, squares[...])

    def basis_step(i):
        acts = [ROUTES[p][i] for p in range(ring)]
        active = pick(me, [a is not None for a in acts])
        acts = [a or IDLE for a in acts]
        steps = got.shape[0] // 2

        @when(active == 1)
        def _():
            row = pick(me, [a[0] for a in acts])
            for side in range(2):
                @when(pick(me, [a[1 + side] for a in acts]) == 1)
                def _(side=side):
                    arrived(got.at[side * steps + i], got_sem.at[side * steps + i])
                    part[row] = part[row] + got[side * steps + i]
            slot = pick(me, [a[4] + (steps if a[3] < 0 else 0) for a in acts])

            @when(pick(me, [a[3] != 0 for a in acts]) == 1)
            def _():
                before = pick(me, [a[5] for a in acts])
                @when(before > 0)
                def _():
                    left_here(part.at[0], send_sem.at[before - 1])
                to = pick(me, [(p + acts[p][3]) % ring for p in range(ring)])
                remote(part.at[row], got.at[slot], send_sem.at[i], got_sem.at[slot], panel=to).start()

            @when(pick(me, [a[3] == 0 for a in acts]) == 1)
            def _():
                roots[pl.ds(pl.multiple_of(slot * half, half), half), :] = part[row]

    def add_gram(n, _):
        x = roots[pl.ds(pl.multiple_of(n * 2 * blk, 2 * blk), 2 * blk), :]
        h, l = split(x)
        th, tl = split(x.T)
        n = 0
        for b in range(3):
            at = slice(b * blk, (b + 1) * blk)
            y = dot(th[at], h[:, b * blk:]) + dot(th[at], l[:, b * blk:]) + dot(tl[at], h[:, b * blk:])
            for j in range(3 - b):
                at = pl.ds(n * blk, blk)
                a_now[at, :] = a_now[at, :] + y[:, j * blk:(j + 1) * blk]
                n += 1
        return 0

    def b_first():
        @when(core == 1)
        def _():
            b_put[0] = link_full[...]
            for h in range(2):
                ship(b_put, b_got, b_send, b_recv, 0, h, tm=mate)
        keep(0, link_full[...])

    def b_pair():
        @when(core == 0)
        def _():
            for h in range(2):
                landed(b_got, b_recv, 0, h)
            x = times_kept(b_got[0], 0)
            keep(1, x)
            if levels > 1:
                b_put[1] = x
        @when(core == 1)
        def _():
            keep_h[1] = keep_h[0]
            keep_l[1] = keep_l[0]
            keep_ht[1] = keep_ht[0]
            keep_lt[1] = keep_lt[0]

    def b_sends(k):
        d = 2 ** k
        return jnp.logical_and(core == 0, jnp.logical_and(m >= d, m + d < chips))

    def b_start(k):
        @when(b_sends(k))
        def _():
            for h in range(2):
                ship(b_put, b_got, b_send, b_recv, k + 1, h, tm=t - 2 ** (k + 1))

    def b_relays(k):
        return jnp.logical_and(core == 0, m + 2 ** (k + 1) < chips)

    def b_end(k, which):
        @when(jnp.logical_and(core == which, m + 2 ** (k + 1) < chips))
        def _():
            relay(b_got, br_send, b_recv, k + 1)
            x = times_kept(b_got[k + 1], k + 1)
            keep(k + 2, x)
            if which == 0 and k + 2 < levels:
                b_put[k + 2] = x

    def partial_rows(n, _):
        at = pl.ds(n * 4 * SPLIT, 4 * SPLIT)
        x = dot(inv[at].reshape(4 * blk, local), spread[...])
        part[at] = x.reshape(4 * SPLIT, half, width)
        return 0
    size = width // ring
    reduce_step(0, link_part, size, link_put, link_got, lr_send, lr_recv)
    lax.fori_loop(0, inv.shape[0] // (4 * SPLIT), partial_rows, 0)
    a_now[...] = jnp.zeros_like(a_now)
    roots[...] = jnp.zeros_like(roots)
    squares[...] = jnp.zeros_like(squares)
    nsteps = got.shape[0] // 2
    nblocks = inv.shape[0]
    extra = {}

    def add(i, f):
        extra.setdefault(i, []).append(f)

    for s in range(1, 4):
        add(LINK_AT[s], functools.partial(reduce_step, s, link_part, size, link_put, link_got, lr_send, lr_recv))
    add(LINK_AT[4], functools.partial(reduce_end, link_part, size, link_got, lr_recv, link_full))
    for s in range(4):
        add(LINK_AT[4 + s], functools.partial(gather_step, s, link_full, size, lg_send, lg_recv))
    first = LINK_AT[8]
    add(first, functools.partial(gather_end, link_full, size, lg_recv))
    add(first, b_first)
    add(first + 1, b_pair)
    if levels > 1:
        add(first + 1, functools.partial(b_start, 0))
        add(first + 6, functools.partial(b_end, 0, 0))
        add(first + 7, functools.partial(b_end, 0, 1))
    if levels > 2:
        add(first + 6, functools.partial(b_start, 1))
    for i, low, high in GRAM_AT:
        add(i, lambda low=low, high=high: lax.fori_loop(pick(me, low), pick(me, high), add_gram, 0))
    for i in range(max(nsteps, max(extra) + 1)):
        for f in extra.get(i, []):
            f()
        if i < nsteps:
            basis_step(i)

    @when(core == 1)
    def _():
        a_put[0] = a_now[...]
        for h in range(2):
            ship(a_put, a_got, a_send, a_recv, 0, h, tm=mate)

    @when(core == 0)
    def _():
        for h in range(2):
            landed(a_got, a_recv, 0, h)
        sandwich(a_got.at[0], 0)

    for k in range(levels):
        d = 2 ** k
        @when(jnp.logical_and(core == 0, m >= d))
        def _(k=k, d=d):
            a_put[k + 1] = a_now[...]
            for h in range(2):
                ship(a_put, a_got, a_send, a_recv, k + 1, h, tm=t - 2 * d)

        if 0 < k and k + 1 < levels:
            b_end(k, 0)
            if k + 2 < levels:
                b_start(k + 1)
        add_squares(k * nblocks // levels, nblocks // levels)

        @when(m + d < chips)
        def _(k=k):
            relay(a_got, ar_send, a_recv, k + 1)
            sandwich(a_got.at[k + 1], k + 1)
        if 0 < k and k + 1 < levels:
            b_end(k, 1)

    size2 = 6 * blk // ring

    def forward(j, at):
        @when(t > 0)
        def _():
            remote(last_full.at[at, :], state.at[at, :], st_send.at[j], st_recv.at[j], tm=t - 1).start()

    spread_start(a_now, size2, last_got, fr_send, fr_recv)
    spread_end(a_now, size2, last_got, fr_recv, last_full)
    share_start(last_full, size2, fg_send, fg_recv)
    forward(0, pl.ds(pl.multiple_of(me * size2, 8), size2))
    share_end(last_full, size2, fg_recv, forward)

    def write_schur(i, j, x):
        schur_out[pl.ds(i * blk, blk), pl.ds(j * blk, blk)] = x
    unpack(last_full, write_schur)

    @when(t + 1 < total_steps)
    def _():
        for d in range(ring):
            r = lax.rem(me + ring - d, ring)
            at = pl.ds(pl.multiple_of(r * size2, 8), size2)
            arrived(state.at[at, :], st_recv.at[d])

    @when(t + 1 == total_steps)
    def _():
        state[...] = jnp.zeros_like(state)

    def write_state(i, j, x):
        h, l = split(x)
        mat_h[pl.ds(i * blk, blk), pl.ds(j * blk, blk)] = h
        mat_l[pl.ds(i * blk, blk), pl.ds(j * blk, blk)] = l
    unpack(state, write_state)
    total = jnp.sum(squares[...], axis=0, keepdims=True)
    y = dot(mat_h[...], picks[...]) + dot(mat_l[...], picks[...])
    var_out[...] = total + jnp.sum(picks[...].astype(F32) * y, axis=0, keepdims=True)

    for i in range(nsteps):
        acts = [ROUTES[p][i] or IDLE for p in range(ring)]
        @when(pick(me, [a[6] for a in acts]) == 1)
        def _(i=i):
            left_here(part.at[0], send_sem.at[i])
    for j in range(ring - 1):
        left_here(link_got.at[j], lr_send.at[j])
        left_here(link_got.at[j], lg_send.at[j])
        left_here(last_got.at[j], fr_send.at[j])
        left_here(last_got.at[j], fg_send.at[j])

    @when(t > 0)
    def _():
        for j in range(ring):
            left_here(last_got.at[0], st_send.at[j])

    @when(core == 1)
    def _():
        shipped(b_got, b_send, 0)
        shipped(a_got, a_send, 0)
    for k in range(levels):
        d = 2 ** k
        if k < levels - 1:
            @when(b_sends(k))
            def _(k=k):
                shipped(b_got, b_send, k + 1)
            @when(b_relays(k))
            def _(k=k):
                shipped(b_got, br_send, k + 1)
        @when(jnp.logical_and(core == 0, m >= d))
        def _(k=k):
            shipped(a_got, a_send, k + 1)
        @when(jnp.logical_and(core == 0, m + d < chips))
        def _(k=k):
            shipped(a_got, ar_send, k + 1)


def per_device(ring, inv_diag, couple, col_blocks, row_blocks):
    nodes, local = inv_diag.shape[1], inv_diag.shape[2]
    blk = couple.shape[3]
    width = couple.shape[1] * blk
    total_steps = col_blocks.shape[0]
    chips = total_steps // 2
    levels = len([d for d in (1, 2, 4, 8, 16) if d < chips])
    nsteps = len(ROUTES[0])
    half = blk // SPLIT
    piece, piece2 = width // ring, 6 * blk // ring
    vm, dma = pltpu.VMEM, pltpu.SemaphoreType.DMA
    packed = (6 * blk, blk)
    scratch = [
        vm((local, width), BF16), vm((width, local), BF16), vm((8, local), F32),
        vm((nodes // half, half, width), F32), vm((2 * blk * max(GRAM_AT[-1][2]), width), F32), vm((2 * nsteps, half, width), F32),
        vm((width, width), F32), vm((width, width), F32), vm((7, piece, width), F32), vm((7, piece, width), F32),
        vm((levels + 1, width, width), BF16), vm((levels + 1, width, width), BF16),
        vm((levels + 1, width, width), BF16), vm((levels + 1, width, width), BF16),
        vm((levels, width, width), F32), vm((levels, width, width), F32),
        vm(packed, F32), vm((levels + 1,) + packed, F32), vm((levels + 1,) + packed, F32),
        vm((width, width), BF16), vm((width, width), BF16), vm((width, width), BF16), vm((width, width), BF16),
        vm((ring - 1, piece2, blk), F32), vm(packed, F32),
        vm(packed, F32), vm((8, 128), F32),
        dma((nsteps,)), dma((2 * nsteps,)),
        *[dma((ring - 1,)) for _ in range(8)],
        dma((ring,)), dma((ring,)),
        dma((levels, 2)), dma((levels, 2)), dma((levels, 2)),
        dma((levels + 1, 2)), dma((levels + 1, 2)), dma((levels + 1, 2)),
    ]
    vmem = pl.BlockSpec(memory_space=pltpu.VMEM)
    smem = pl.BlockSpec(memory_space=pltpu.SMEM)
    variances, schur = pl.pallas_call(
        functools.partial(kernel, ring, total_steps),
        out_shape=(jax.ShapeDtypeStruct((1, local), F32), jax.ShapeDtypeStruct((width, width), F32)),
        in_specs=[vmem, vmem, smem, smem],
        out_specs=(vmem, vmem),
        scratch_shapes=scratch,
        compiler_params=pltpu.CompilerParams(
            collective_id=0, has_side_effects=True, vmem_limit_bytes=56 * 1024 * 1024
        ),
        name="sweep",
    )(inv_diag[0].reshape(nodes // half, half, local), couple[0], col_blocks, row_blocks)
    return variances, schur[None]


def solution(mesh):
    return jax.shard_map(
        functools.partial(per_device, mesh.shape["panel"]),
        mesh=mesh,
        in_specs=(P("tm", None, "panel"), P("tm", None, None, None, None), P(), P("tm", None)),
        out_specs=(P("tm", "panel"), P("tm", None, None)),
        check_vma=False,
    )
```

time: 160 us -> 147 us (0.919)
  the two profiles are of different devices: /device:TPU:35 before, /device:TPU:45 now
where the time goes in v2:
time: 147 us
  Pallas kernels  142 us (97%)
  local copies, waits for them, and re-layouts  4.54 us (3%)
    pallas_call x1, Pallas kernels, per_device(): pl.pallas_call(functools.partial(kernel, ring, total_steps), out_shape=(j...  142 us
    unnamed x3, local copies, waits for them, and re-layouts  4.54 us

profile of v2, /device:TPU:45, one launch (start us, length us, event | category | flops | bytes accessed | tf_op | source)
XLA Modules:
  0.0 147.0 jit_solution(5633960908712139325)
XLA Ops:
  0.6 1.4 copy.6.cols
  2.0 141.9 %sweep.1 = (f32[1,512]{1,0:T(1,128)}, f32[384,384]{1,0:T(8,128)}) custom-call(bf16[32,128,512]{2,1,0:T(8,128)(2,1)} %bitcast.3, bf16[3,4,128,128]{3,2,1,0:T(8,128)(2,1)} %bitcast.5, s32[32,3]{1,0:T(8,128)} %copy.6.cols, s32[1,4]{1,0:T(1,128)} %rows.1), custom_call_target="tpu_custom_call" | custom-call | tf_op jit(solution)/shard_map/sweep/pallas_call | solution.py:600
  143.9 1.3 copy.9
  145.1 1.9 %copy.10 = f32[1,384,384]{2,1,0:T(8,128)} copy(f32[1,384,384]{2,1,0:T(8,128)} %bitcast.4) | data formatting | bytes 1179648

commit v3 on v2

--- a/solution.py
+++ b/solution.py
@@ -101,7 +101,8 @@
     (21, (3, 1, 0, 0, 0, 0, 0, 0), (3, 2, 0, 0, 0, 0, 0, 0)),
     (26, (3, 2, 0, 0, 0, 0, 0, 0), (4, 3, 1, 0, 0, 0, 0, 0)),
     (29, (4, 3, 1, 0, 0, 0, 0, 0), (4, 3, 2, 1, 0, 1, 0, 1)),
-    (32, (4, 3, 2, 1, 0, 1, 0, 1), (6, 4, 2, 1, 1, 1, 1, 1)),
+    (31, (4, 3, 2, 1, 0, 1, 0, 1), (5, 4, 2, 1, 0, 1, 0, 1)),
+    (32, (5, 4, 2, 1, 0, 1, 0, 1), (6, 4, 2, 1, 1, 1, 1, 1)),
 )
 IDLE = (0, 0, 0, 0, 0, 0, 0)
 PAIRS = ((0, 0), (0, 1), (0, 2), (1, 1), (1, 2), (2, 2))
@@ -132,10 +133,10 @@
     return high, (x - high.astype(F32)).astype(BF16)
 
 
-def kernel(ring, total_steps, inv, couple, cols, rows, var_out, schur_out, spread, picks, squares,
+def kernel(ring, total_steps, inv, couple, cols, rows, var_out, last_full, spread, picks, squares,
            part, roots, got, link_part, link_full, link_put, link_got, keep_h, keep_l, keep_ht, keep_lt,
-           b_put, b_got, a_now, a_put, a_got, mat_h, mat_l, tmp_h, tmp_l, last_got, last_full,
-           state, state_full, send_sem, got_sem, lr_send, lr_recv, lg_send, lg_recv, fr_send, fr_recv,
+           b_put, b_got, a_now, a_put, a_got, mat_h, mat_l, tmp_h, tmp_l, last_got,
+           state, send_sem, got_sem, lr_send, lr_recv, lg_send, lg_recv, fr_send, fr_recv,
            fg_send, fg_recv, st_send, st_recv, b_send, b_recv, br_send, a_send, a_recv, ar_send):
     me = lax.axis_index("panel")
     t = lax.axis_index("tm")
@@ -235,7 +236,7 @@
             arrived(dest.at[at, :], rsem.at[3 + 3 * way])
 
     def spread_start(source, size, recv, ssem, rsem):
-        for d in range(1, ring):
+        for d in (4, 3, 5, 2, 6, 1, 7):
             r = lax.rem(me + d, ring)
             src = source.at[pl.ds(pl.multiple_of(r * size, 8), size), :]
             remote(src, recv.at[d - 1], ssem.at[d - 1], rsem.at[d - 1], panel=r).start()
@@ -275,12 +276,20 @@
         for h in range(2):
             left_here(src.at[n, halves(src.shape[1])[h], :], ssem.at[n, h])
 
-    def relay(buf, ssem, rsem, n):
+    def relay(buf, ssem, rsem, n, then=None):
         for h in range(2):
             landed(buf, rsem, n, h)
             @when(core == 0)
             def _(h=h):
                 ship(buf, buf, ssem, rsem, n, h, tm=mate)
+            if then is not None:
+                then(h)
+
+    def sandwich_half(n, v, h):
+        if h == 0:
+            sandwich(a_got.at[n], v, 0, range(3), 0, blk)
+        else:
+            sandwich(a_got.at[n], v, 1, range(3, 6), blk, 2 * blk)
 
     def keep(v, x):
         h, l = split(x)
@@ -295,23 +304,27 @@
         h, l = split(x)
         return dot(h, keep_h[v]) + dot(h, keep_l[v]) + dot(l, keep_h[v])
 
-    def unpack(src, write):
-        for n, (i, j) in enumerate(PAIRS):
+    def unpack(src, write, blocks=range(6)):
+        for n in blocks:
+            i, j = PAIRS[n]
             x = src[pl.ds(n * blk, blk), :]
             write(i, j, x)
             if i != j:
                 write(j, i, x.T)
 
-    def sandwich(src, v):
+    def sandwich(src, v, part, blocks, top, count):
         def write(i, j, x):
             h, l = split(x)
             mat_h[pl.ds(i * blk, blk), pl.ds(j * blk, blk)] = h
             mat_l[pl.ds(i * blk, blk), pl.ds(j * blk, blk)] = l
-        unpack(src, write)
-        x = dot(mat_h[...], keep_h[v]) + dot(mat_h[...], keep_l[v]) + dot(mat_l[...], keep_h[v])
+        unpack(src, write, blocks)
+        at = pl.ds(top, count)
+        x = dot(mat_h[at, :], keep_h[v]) + dot(mat_h[at, :], keep_l[v]) + dot(mat_l[at, :], keep_h[v])
         h, l = split(x)
-        tmp_h[...] = h
-        tmp_l[...] = l
+        tmp_h[at, :] = h
+        tmp_l[at, :] = l
+        if part == 0:
+            return
         n = 0
         for i in range(3):
             rows_i = pl.ds(i * blk, blk)
@@ -469,7 +482,7 @@
     def _():
         for h in range(2):
             landed(a_got, a_recv, 0, h)
-        sandwich(a_got.at[0], 0)
+            sandwich_half(0, 0, h)
 
     for k in range(levels):
         d = 2 ** k
@@ -487,8 +500,7 @@
 
         @when(m + d < chips)
         def _(k=k):
-            relay(a_got, ar_send, a_recv, k + 1)
-            sandwich(a_got.at[k + 1], k + 1)
+            relay(a_got, ar_send, a_recv, k + 1, functools.partial(sandwich_half, k + 1, k + 1))
         if 0 < k and k + 1 < levels:
             b_end(k, 1)
 
@@ -504,10 +516,6 @@
     share_start(last_full, size2, fg_send, fg_recv)
     forward(0, pl.ds(pl.multiple_of(me * size2, 8), size2))
     share_end(last_full, size2, fg_recv, forward)
-
-    def write_schur(i, j, x):
-        schur_out[pl.ds(i * blk, blk), pl.ds(j * blk, blk)] = x
-    unpack(last_full, write_schur)
 
     @when(t + 1 < total_steps)
     def _():
@@ -564,6 +572,16 @@
         @when(jnp.logical_and(core == 0, m + d < chips))
         def _(k=k):
             shipped(a_got, ar_send, k + 1)
+
+
+def finish(var, last, var_out, schur_out):
+    blk = last.shape[1]
+    var_out[...] = var[...]
+    for n, (i, j) in enumerate(PAIRS):
+        x = last[pl.ds(n * blk, blk), :]
+        schur_out[pl.ds(i * blk, blk), pl.ds(j * blk, blk)] = x
+        if i != j:
+            schur_out[pl.ds(j * blk, blk), pl.ds(i * blk, blk)] = x.T
 
 
 def per_device(ring, inv_diag, couple, col_blocks, row_blocks):
@@ -587,8 +605,8 @@
         vm((levels, width, width), F32), vm((levels, width, width), F32),
         vm(packed, F32), vm((levels + 1,) + packed, F32), vm((levels + 1,) + packed, F32),
         vm((width, width), BF16), vm((width, width), BF16), vm((width, width), BF16), vm((width, width), BF16),
-        vm((ring - 1, piece2, blk), F32), vm(packed, F32),
-        vm(packed, F32), vm((8, 128), F32),
+        vm((ring - 1, piece2, blk), F32),
+        vm(packed, F32),
         dma((nsteps,)), dma((2 * nsteps,)),
         *[dma((ring - 1,)) for _ in range(8)],
         dma((ring,)), dma((ring,)),
@@ -597,9 +615,9 @@
     ]
     vmem = pl.BlockSpec(memory_space=pltpu.VMEM)
     smem = pl.BlockSpec(memory_space=pltpu.SMEM)
-    variances, schur = pl.pallas_call(
+    variances, last = pl.pallas_call(
         functools.partial(kernel, ring, total_steps),
-        out_shape=(jax.ShapeDtypeStruct((1, local), F32), jax.ShapeDtypeStruct((width, width), F32)),
+        out_shape=(jax.ShapeDtypeStruct((1, local), F32), jax.ShapeDtypeStruct(packed, F32)),
         in_specs=[vmem, vmem, smem, smem],
         out_specs=(vmem, vmem),
         scratch_shapes=scratch,
@@ -608,6 +626,13 @@
         ),
         name="sweep",
     )(inv_diag[0].reshape(nodes // half, half, local), couple[0], col_blocks, row_blocks)
+    variances, schur = pl.pallas_call(
+        finish,
+        out_shape=(jax.ShapeDtypeStruct((1, local), F32), jax.ShapeDtypeStruct((width, width), F32)),
+        in_specs=[vmem, vmem],
+        out_specs=(vmem, vmem),
+        name="finish",
+    )(variances, last)
     return variances, schur[None]
 
 

time: 147 us -> 145 us (0.986)
  local copies, waits for them, and re-layouts: 4.54 us -> 1.37 us
    unnamed x3 -> x1, local copies, waits for them, and re-layouts: 4.54 us -> 1.37 us
    pallas_call x0 -> x1, Pallas kernels: none -> 1.95 us  [per_device(): pl.pallas_call(finish, out_shape=(jax.ShapeDtypeStruct((1, local), F32),...]
where the time goes in v3:
time: 145 us
  Pallas kernels  143 us (99%)
    pallas_call x1, Pallas kernels, per_device(): pl.pallas_call(functools.partial(kernel, ring, total_steps), out_shape=(j...  141 us

profile of v3, /device:TPU:45, one launch (start us, length us, event | category | flops | bytes accessed | tf_op | source)
XLA Modules:
  0.0 144.7 jit_solution(3161336431125479702)
XLA Ops:
  0.6 1.4 copy.6.cols
  2.0 140.7 %sweep.1 = (f32[1,512]{1,0:T(1,128)}, f32[768,128]{1,0:T(8,128)}) custom-call(bf16[32,128,512]{2,1,0:T(8,128)(2,1)} %bitcast.3, bf16[3,4,128,128]{3,2,1,0:T(8,128)(2,1)} %bitcast.4, s32[32,3]{1,0:T(8,128)} %copy.6.cols, s32[1,4]{1,0:T(1,128)} %rows.1), custom_call_target="tpu_custom_call" | custom-call | tf_op jit(solution)/shard_map/sweep/pallas_call | solution.py:618
  142.8 2.0 %finish.1 = (f32[1,512]{1,0:T(1,128)}, f32[384,384]{1,0:T(8,128)}) custom-call(f32[1,512]{1,0:T(1,128)} %get-tuple-element.6.var, f32[768,128]{1,0:T(8,128)} %get-tuple-element.7.last), custom_call_target="tpu_custom_call" | custom-call | tf_op jit(solution)/shard_map/finish/pallas_call | solution.py:629

commit v4 on v3

--- a/solution.py
+++ b/solution.py
@@ -285,11 +285,11 @@
             if then is not None:
                 then(h)
 
-    def sandwich_half(n, v, h):
+    def sandwich_half(n, v, early, h):
         if h == 0:
             sandwich(a_got.at[n], v, 0, range(3), 0, blk)
         else:
-            sandwich(a_got.at[n], v, 1, range(3, 6), blk, 2 * blk)
+            sandwich(a_got.at[n], v, 1, range(3, 6), blk, 2 * blk, early)
 
     def keep(v, x):
         h, l = split(x)
@@ -312,7 +312,7 @@
             if i != j:
                 write(j, i, x.T)
 
-    def sandwich(src, v, part, blocks, top, count):
+    def sandwich(src, v, part, blocks, top, count, early=None):
         def write(i, j, x):
             h, l = split(x)
             mat_h[pl.ds(i * blk, blk), pl.ds(j * blk, blk)] = h
@@ -335,6 +335,8 @@
                 at = pl.ds(n * blk, blk)
                 a_now[at, :] = a_now[at, :] + x[:, j * blk:(j + 1) * blk]
                 n += 1
+            if i == 0 and early is not None:
+                early()
 
     def add_squares(first, count):
         def one(n, total):
@@ -472,6 +474,17 @@
         if i < nsteps:
             basis_step(i)
 
+    def a_ship(k, h):
+        @when(jnp.logical_and(core == 0, m >= 2 ** k))
+        def _():
+            at = halves(6 * blk)[h]
+            a_put[k + 1, at, :] = a_now[at, :]
+            ship(a_put, a_got, a_send, a_recv, k + 1, h, tm=t - 2 ** (k + 1))
+
+    def a_early(k):
+        if k < levels:
+            a_ship(k, 0)
+
     @when(core == 1)
     def _():
         a_put[0] = a_now[...]
@@ -482,15 +495,15 @@
     def _():
         for h in range(2):
             landed(a_got, a_recv, 0, h)
-            sandwich_half(0, 0, h)
+            sandwich_half(0, 0, functools.partial(a_early, 0), h)
 
     for k in range(levels):
         d = 2 ** k
-        @when(jnp.logical_and(core == 0, m >= d))
-        def _(k=k, d=d):
-            a_put[k + 1] = a_now[...]
-            for h in range(2):
-                ship(a_put, a_got, a_send, a_recv, k + 1, h, tm=t - 2 * d)
+        if k > 0:
+            @when(m + d // 2 >= chips)
+            def _(k=k):
+                a_early(k)
+        a_ship(k, 1)
 
         if 0 < k and k + 1 < levels:
             b_end(k, 0)
@@ -500,7 +513,7 @@
 
         @when(m + d < chips)
         def _(k=k):
-            relay(a_got, ar_send, a_recv, k + 1, functools.partial(sandwich_half, k + 1, k + 1))
+            relay(a_got, ar_send, a_recv, k + 1, functools.partial(sandwich_half, k + 1, k + 1, functools.partial(a_early, k + 1)))
         if 0 < k and k + 1 < levels:
             b_end(k, 1)
 

time: 145 us -> 145 us (level)
  no operation moved by 1% of the time
where the time goes in v4:
time: 145 us
  Pallas kernels  143 us (99%)
    pallas_call x1, Pallas kernels, per_device(): pl.pallas_call(functools.partial(kernel, ring, total_steps), out_shape=(j...  141 us

profile of v4, /device:TPU:45, one launch (start us, length us, event | category | flops | bytes accessed | tf_op | source)
XLA Modules:
  0.0 144.9 jit_solution(596860897034928745)
XLA Ops:
  0.6 1.4 copy.6.cols
  2.0 140.9 %sweep.1 = (f32[1,512]{1,0:T(1,128)}, f32[768,128]{1,0:T(8,128)}) custom-call(bf16[32,128,512]{2,1,0:T(8,128)(2,1)} %bitcast.3, bf16[3,4,128,128]{3,2,1,0:T(8,128)(2,1)} %bitcast.4, s32[32,3]{1,0:T(8,128)} %copy.6.cols, s32[1,4]{1,0:T(1,128)} %rows.1), custom_call_target="tpu_custom_call" | custom-call | tf_op jit(solution)/shard_map/sweep/pallas_call | solution.py:631
  142.9 2.0 %finish.1 = (f32[1,512]{1,0:T(1,128)}, f32[384,384]{1,0:T(8,128)}) custom-call(f32[1,512]{1,0:T(1,128)} %get-tuple-element.6.var, f32[768,128]{1,0:T(8,128)} %get-tuple-element.7.last), custom_call_target="tpu_custom_call" | custom-call | tf_op jit(solution)/shard_map/finish/pallas_call | solution.py:642
